TPU v7x, 128 devices: a whole 4x4x4 slice. The times are simulated.
128 devices in a mesh: step: 8 (over z, x_hi), tok: 16 (over y, x_lo, core).
Axes of the slice: x: 4 (x_hi: 2, x_lo: 2; x = x_hi * 2 + x_lo), y: 4, z: 4, core: 2. Of those that a mesh axis runs over, the one named last changes fastest.
Arguments:
- latents: bfloat16 [8, 8192, 1152], P('step', 'tok'), may hold values from -6 to 6
- timesteps: int32 [32], replicated, may hold values from 0 to 63
- experts: int32 [32], replicated, may hold values from 0 to 1
- offset: int32 [1], replicated, may hold values from 0 to 24
- modulation: float32 [64, 3, 1152], replicated, may hold values from -4 to 4
- coef: float32 [64], replicated, may hold values from 0.1 to 1
- w_qkv: bfloat16 [2, 1152, 16, 216], P(None, None, 'tok'), may hold values from -1 to 1
- w_o: bfloat16 [2, 1152, 1152], P(None, 'tok'), may hold values from -0.1875 to 0.1875
- w_cq: bfloat16 [2, 1152, 1152], P(None, None, 'tok'), may hold values from -0.1875 to 0.1875
- w_co: bfloat16 [2, 1152, 1152], P(None, 'tok'), may hold values from -0.1875 to 0.1875
- text_kv: bfloat16 [2, 2, 300, 1152], replicated, may hold values from -240 to 240
Outputs:
- new_latents: bfloat16 [8, 8192, 1152], P('step', 'tok')
All inputs are finite; a program needn't handle non-finite values.
Results may differ from a plain program's by a relative error of at most 0.028.
The roundings to bfloat16 on the way count: a program that leaves them out, or rounds other values in their place, can miss the bound.
Values may be sent and summed in bfloat16 or wider, within the bound.
No kernel may reach another device: no remote copies, remote signals or barrier semaphores. Data moves between devices by JAX's collectives and lax.ppermute only.
A program may use at most 128 MiB of HBM per device.

v0:
```python
import functools
import math

import jax
import jax.numpy as jnp
from jax import lax
from jax.experimental import pallas as pl
from jax.experimental.pallas import tpu as pltpu
from jax.sharding import PartitionSpec as P

HEAD = 72
LANES = 128
TEXT = 300
TEXT_PAD = 384
CHUNKS = (384, 128)
SOURCES = (4, 8)
ROW_BLOCK = 1024
ROWS = 128
KEY_BLOCK = 1024
HALVES = 2
VALUE = 2 * HEAD - LANES
FACTOR = math.log2(math.e) / HEAD**0.5
VMEM_LIMIT = 60 * 2**20
def link_kernel(passed, *refs):
    del passed, refs


def link(values, after):
    values = list(values)
    return pl.pallas_call(
        functools.partial(link_kernel, len(values)),
        in_specs=[pl.BlockSpec(memory_space=pl.ANY)] * (len(values) + len(after)),
        out_specs=[pl.BlockSpec(memory_space=pl.ANY)] * len(values),
        out_shape=[jax.ShapeDtypeStruct(value.shape, value.dtype) for value in values],
        input_output_aliases={index: index for index in range(len(values))},
        compiler_params=pltpu.CompilerParams(vmem_limit_bytes=VMEM_LIMIT),
        name="link",
    )(*values, *after)


def whole(array):
    return pl.BlockSpec(array.shape, lambda *_: (0,) * len(array.shape))


def norm_kernel(entry, latent, modulation, *outs):
    flat = latent[...].astype(jnp.float32)
    mean = jnp.mean(flat, axis=1, keepdims=True)
    centred = flat - mean
    var = jnp.mean(centred**2, axis=1, keepdims=True)
    row = pl.ds(entry[0] % 8, 1)
    shift, scale = modulation[0, row, :], modulation[1, row, :]
    normed = (centred * lax.rsqrt(var + 1e-06) * (1.0 + scale) + shift).astype(jnp.bfloat16)
    here = pl.program_id(0)
    first = CHUNKS[0] // ROWS

    @pl.when(here < first)
    def _():
        outs[0][...] = normed

    @pl.when(here >= first)
    def _():
        outs[1][...] = normed


def norm(latent, modulation, entry):
    count, width = latent.shape
    first = CHUNKS[0] // ROWS
    block = (ROWS, width)
    return pl.pallas_call(
        norm_kernel,
        grid_spec=pltpu.PrefetchScalarGridSpec(
            num_scalar_prefetch=1,
            grid=(count // ROWS,),
            in_specs=[
                pl.BlockSpec(block, lambda i, entry: (i, 0)),
                pl.BlockSpec((3, 8, width), lambda i, entry: (0, entry[0] // 8, 0)),
            ],
            out_specs=[
                pl.BlockSpec(block, lambda i, entry: (jnp.minimum(i, first - 1), 0)),
                pl.BlockSpec(block, lambda i, entry: (jnp.maximum(i - first, 0), 0)),
            ],
        ),
        out_shape=[jax.ShapeDtypeStruct((per, width), jnp.bfloat16) for per in CHUNKS],
        compiler_params=pltpu.CompilerParams(vmem_limit_bytes=VMEM_LIMIT),
        name="norm",
    )(entry, latent, modulation)


def project_kernel(waited, *refs):
    rows, weights, queries, keys, values = refs[waited:]
    mixed = jnp.dot(rows[...], weights[...], preferred_element_type=jnp.float32)
    low, high = mixed[:, :LANES], mixed[:, LANES:]
    queries[...] = low.astype(jnp.bfloat16)
    lane = lax.broadcasted_iota(jnp.int32, high.shape, 1)
    values[...] = jnp.where(lane >= VALUE + HEAD, 1.0, high).astype(jnp.bfloat16)
    pad = jnp.zeros((LANES - HEAD, mixed.shape[0]), jnp.float32)
    keys[...] = jnp.concatenate([low.T[HEAD:], high.T[:VALUE], pad], 0).astype(jnp.bfloat16)


def project(tokens, weights, after):
    count, width = tokens.shape
    flat = jax.ShapeDtypeStruct((count, LANES), jnp.bfloat16)
    turned = jax.ShapeDtypeStruct((LANES, count), jnp.bfloat16)
    flat_spec = pl.BlockSpec((ROW_BLOCK, LANES), lambda i: (i, 0))
    return pl.pallas_call(
        functools.partial(project_kernel, len(after)),
        grid=(count // ROW_BLOCK,),
        in_specs=[pl.BlockSpec(memory_space=pl.ANY)] * len(after)
        + [pl.BlockSpec((ROW_BLOCK, width), lambda i: (i, 0)), whole(weights)],
        out_specs=[flat_spec, pl.BlockSpec((LANES, ROW_BLOCK), lambda i: (0, i)), flat_spec],
        out_shape=(flat, turned, flat),
        compiler_params=pltpu.CompilerParams(vmem_limit_bytes=VMEM_LIMIT),
        cost_estimate=pl.CostEstimate(
            flops=4 * count * width * LANES,
            bytes_accessed=count * width * 2 + count * 6 * LANES,
            transcendentals=0,
        ),
        name="project",
    )(*after, tokens, weights)


def attend_kernel(waited, key_chunks, carried, final, *refs):
    refs = list(refs)[waited:]
    query_ref = refs.pop(0)
    keys = refs[:key_chunks]
    values = refs[key_chunks : 2 * key_chunks]
    del refs[: 2 * key_chunks]
    state = refs.pop(0) if carried else None
    out, scores = refs
    parts = [
        (key, value, slice(start, start + KEY_BLOCK))
        for key, value in zip(keys, values)
        for start in range(0, key.shape[1], KEY_BLOCK)
    ]
    rows = query_ref.shape[0] // HALVES
    spans = [slice(half * rows, (half + 1) * rows) for half in range(HALVES)]
    units = [(half, step) for step in range(len(parts)) for half in range(HALVES)]

    def score(unit):
        half, step = unit
        key, _, span = parts[step]
        return jnp.dot(
            query_ref[spans[half], :], key[:, span], preferred_element_type=jnp.float32
        )

    totals = [state[span, :] if carried else None for span in spans]
    tops = [total[:, LANES - 1 :] if carried else None for total in totals]
    scores[0] = score(units[0])
    for index, (half, step) in enumerate(units):
        if index + 1 < len(units):
            scores[(index + 1) % 2] = score(units[index + 1])
        now = scores[index % 2]
        top, total = tops[half], totals[half]
        high = jnp.max(now, axis=1, keepdims=True)
        newer = high if top is None else jnp.maximum(top, high)
        weights = jnp.exp2(now * FACTOR - newer * FACTOR).astype(jnp.bfloat16)
        _, value, span = parts[step]
        part = jnp.dot(weights, value[span, :], preferred_element_type=jnp.float32)
        totals[half] = part if top is None else total * jnp.exp2((top - newer) * FACTOR) + part
        tops[half] = newer
    for half, (total, top) in enumerate(zip(totals, tops)):
        if final:
            turned = total.T
            done = turned[VALUE : VALUE + HEAD] / turned[VALUE + HEAD : VALUE + HEAD + 1]
            per = out.shape[2]
            for piece in range(rows // per):
                out[half * (rows // per) + piece] = done[
                    :, piece * per : (piece + 1) * per
                ].astype(jnp.bfloat16)
        else:
            lane = lax.broadcasted_iota(jnp.int32, total.shape, 1)
            out[spans[half], :] = jnp.where(lane == LANES - 1, top, total)


def attend_chunk(queries, per, together, sources, state, final, after):
    count = queries.shape[0]
    block = per * together
    row_spec = pl.BlockSpec((block, LANES), lambda i: (i, 0))
    args = [*after, queries]
    in_specs = [pl.BlockSpec(memory_space=pl.ANY)] * len(after) + [row_spec]
    for index in (1, 2):
        args += [chunk[index] for chunk in sources]
        in_specs += [whole(chunk[index]) for chunk in sources]
    if state is not None:
        args.append(state)
        in_specs.append(row_spec)
    if final:
        out_shape = jax.ShapeDtypeStruct((count // per, HEAD, per), jnp.bfloat16)
        out_spec = pl.BlockSpec((together, HEAD, per), lambda i: (i, 0, 0))
    else:
        out_shape = jax.ShapeDtypeStruct((count, LANES), jnp.float32)
        out_spec = row_spec
    pairs = count * sum(chunk[1].shape[1] for chunk in sources)
    return pl.pallas_call(
        functools.partial(attend_kernel, len(after), len(sources), state is not None, final),
        grid=(count // block,),
        in_specs=in_specs,
        out_specs=out_spec,
        scratch_shapes=[
            pltpu.VMEM((2, block // HALVES, KEY_BLOCK), jnp.float32),
        ],
        out_shape=out_shape,
        compiler_params=pltpu.CompilerParams(vmem_limit_bytes=VMEM_LIMIT),
        cost_estimate=pl.CostEstimate(
            flops=4 * pairs * LANES * 2, bytes_accessed=4 * 2**20, transcendentals=pairs
        ),
        name="self_attend",
    )(*args)


def self_attend(normed, weights, early):
    chunks, states, previous = [], [], []
    held = None
    for chunk in range(len(CHUNKS)):
        own = normed[chunk]
        if held is not None:
            own = link([own], [held] + early[chunk])[0]
        held = lax.all_gather(own, "tok", axis=0, tiled=True)
        chunks.append([held])
    for chunk in range(len(CHUNKS)):
        last = chunk + 1 == len(CHUNKS)
        chunks[chunk] = project(chunks[chunk][0], weights, previous)
        for earlier in range(chunk + 1):
            before = states[earlier] if earlier < chunk else None
            keys = chunks[chunk : chunk + 1] if earlier < chunk else chunks[: chunk + 1]
            result = attend_chunk(
                chunks[earlier][0], CHUNKS[earlier], SOURCES[earlier], keys, before, last, previous
            )
            previous = [result]
            states[earlier : earlier + 1] = [result]
    return states, chunks


def finish_kernel(parts, *refs):
    turned, (latent, mix, weights, keys, values) = refs[:parts], refs[parts : parts + 5]
    out, cross, near, arrived = refs[parts + 5 :]
    width = latent.shape[1]
    copies = [
        pltpu.make_async_copy(weights.at[:, index], near.at[index], arrived.at[index])
        for index in range(3)
    ]
    for copy in copies:
        copy.start()

    def weight(index):
        copies[index].wait()
        return near[index].astype(jnp.float32).reshape(width, width).astype(jnp.bfloat16)

    attended = jnp.concatenate([part[...].astype(jnp.float32) for part in turned], 1)
    attended = attended.T.astype(jnp.bfloat16)
    projected = jnp.dot(attended, weight(0), preferred_element_type=jnp.float32)
    hidden = (latent[...].astype(jnp.float32) + mix[:1, :] * projected).astype(jnp.bfloat16)
    queries = lax.dot_general(
        weight(1), hidden, (((1,), (1,)), ((), ())), preferred_element_type=jnp.float32
    )
    for head in range(width // HEAD):
        rows = slice(head * HEAD, (head + 1) * HEAD)
        scores = jnp.dot(
            keys[head], queries[rows].astype(jnp.bfloat16), preferred_element_type=jnp.float32
        )
        row = lax.broadcasted_iota(jnp.int32, scores.shape, 0)
        scores = jnp.where(row < TEXT, scores, -jnp.inf)
        high = jnp.max(scores, axis=0, keepdims=True)
        exps = jnp.exp2((scores - high) * FACTOR)
        total = jnp.sum(exps, axis=0, keepdims=True)
        result = jnp.dot(
            values[head], exps.astype(jnp.bfloat16), preferred_element_type=jnp.float32
        )
        cross[rows, :] = result / total
    crossed = cross[...].T.astype(jnp.bfloat16)
    predicted = (
        hidden.astype(jnp.float32)
        + jnp.dot(crossed, weight(2), preferred_element_type=jnp.float32)
    ).astype(jnp.bfloat16)
    out[...] = (
        mix[1:2, :] * latent[...].astype(jnp.float32)
        + mix[2:3, :] * predicted.astype(jnp.float32)
    ).astype(jnp.bfloat16)


def finish(turned, latent, mix, weights, keys, values):
    count, width = latent.shape
    heads = width // HEAD
    args = (*turned, latent, mix, weights, keys, values)
    return pl.pallas_call(
        functools.partial(finish_kernel, len(turned)),
        grid=(1,),
        in_specs=[
            pl.BlockSpec(memory_space=pl.ANY) if arg is weights else whole(arg) for arg in args
        ],
        out_specs=whole(latent),
        out_shape=jax.ShapeDtypeStruct((count, width), jnp.bfloat16),
        scratch_shapes=[
            pltpu.VMEM((width, count), jnp.float32),
            pltpu.VMEM((3, heads, HEAD, width), jnp.bfloat16),
            pltpu.SemaphoreType.DMA((3,)),
        ],
        compiler_params=pltpu.CompilerParams(vmem_limit_bytes=VMEM_LIMIT),
        cost_estimate=pl.CostEstimate(
            flops=10 * count * width * width, bytes_accessed=10 * 2**20, transcendentals=0
        ),
        name="finish",
    )(*args)


def scan_kernel(coefs, everyone, out):
    out[0] = everyone[0]
    running = everyone[0].astype(jnp.float32)
    for step in range(1, everyone.shape[0]):
        running = running + coefs[step] * everyone[step].astype(jnp.float32)
        out[step] = running.astype(jnp.bfloat16)


def scan(coefs, everyone):
    return pl.pallas_call(
        scan_kernel,
        grid_spec=pltpu.PrefetchScalarGridSpec(
            num_scalar_prefetch=1,
            grid=(),
            in_specs=[pl.BlockSpec(memory_space=pltpu.VMEM)],
            out_specs=pl.BlockSpec(memory_space=pltpu.VMEM),
        ),
        out_shape=jax.ShapeDtypeStruct(everyone.shape, jnp.bfloat16),
        compiler_params=pltpu.CompilerParams(vmem_limit_bytes=16 * 2**20),
        name="scan",
    )(coefs, everyone)


def body(latents, timesteps, experts, offset, modulation, coef, w_qkv, w_o, w_cq, w_co, text_kv):
    step_index = lax.axis_index("step")
    steps = lax.axis_size("step")
    position = offset[0] + step_index
    entry = lax.dynamic_index_in_dim(timesteps, position, 0, False)
    expert = lax.dynamic_index_in_dim(experts, position, 0, False)
    modulate = lax.dynamic_index_in_dim(modulation, entry, 0, False)
    latent = latents[0]
    count, width = latent.shape
    heads = width // HEAD
    normed = norm(latent, jnp.swapaxes(modulation, 0, 1), entry[None])
    own_qkv = lax.dynamic_index_in_dim(w_qkv, expert, 0, False)[:, 0, :]
    w_mixed = jnp.pad(own_qkv, ((0, 0), (0, 2 * LANES - 3 * HEAD)))

    def over_steps(value):
        shaped = value.reshape(steps, -1, width)
        return lax.all_to_all(shaped, "step", split_axis=0, concat_axis=0, tiled=True)

    own_text = lax.dynamic_index_in_dim(text_kv, expert, 0, False).reshape(2, TEXT, heads, HEAD)
    text_keys = jnp.pad(
        jnp.transpose(own_text[0], (1, 0, 2)), ((0, 0), (0, TEXT_PAD - TEXT), (0, 0))
    )
    text_values = jnp.pad(
        jnp.transpose(own_text[1], (1, 2, 0)), ((0, 0), (0, 0), (0, TEXT_PAD - TEXT))
    )
    text_keys, text_values = link([text_keys, text_values], [])
    own_weights = jnp.stack(
        [
            lax.dynamic_index_in_dim(w_o, expert, 0, False),
            jnp.swapaxes(lax.dynamic_index_in_dim(w_cq, expert, 0, False), 0, 1),
            lax.dynamic_index_in_dim(w_co, expert, 0, False),
        ]
    )
    coefs = jnp.take(coef, lax.dynamic_slice_in_dim(timesteps, offset[0], steps))
    leads = step_index == 0
    mix = jnp.stack(
        [
            modulate[2],
            jnp.full((width,), jnp.where(leads, 1.0, 0.0)),
            jnp.full((width,), jnp.where(leads, coefs[0], 1.0)),
        ]
    )
    heads_out, chunks = self_attend(
        normed, w_mixed, ([], [text_keys, text_values, own_weights, w_mixed, mix])
    )
    all_weights = lax.all_gather(
        link([own_weights], [chunks[0][0]])[0], "tok", axis=0, tiled=False
    )

    def returned(value):
        back = lax.all_to_all(value, "tok", split_axis=0, concat_axis=0, tiled=True)
        return back.reshape(width, -1)

    turned = [returned(heads_out[0])]
    turned.append(returned(link([heads_out[1]], [turned[0], all_weights])[0]))
    sent = finish(turned, latent, mix, all_weights, text_keys, text_values)
    return over_steps(scan(coefs, over_steps(sent))).reshape(1, count, width)


def solution(mesh):
    in_specs = (
        P("step", "tok", None),
        P(),
        P(),
        P(),
        P(),
        P(),
        P(None, None, "tok", None),
        P(None, "tok", None),
        P(None, None, "tok"),
        P(None, "tok", None),
        P(),
    )
    out_specs = P("step", "tok", None)
    return jax.shard_map(body, mesh=mesh, in_specs=in_specs, out_specs=out_specs, check_vma=False)
```

profile of v0, /device:TPU:0, one launch (start us, length us, event | category | flops | bytes accessed | tf_op | source)
XLA Modules:
  0.0 295.9 jit_solution(2332493393514048353)
XLA Ops:
  6.5 0.0 copy-start
  6.5 0.0 all-gather.5.cloned.1.call-start
  7.3 1.3 dynamic_slice.34.entry
  8.6 4.8 %norm.1 = (bf16[384,1152]{1,0:T(8,128)(2,1)}, bf16[128,1152]{1,0:T(8,128)(2,1)}) custom-call(s32[1]{0:T(128)} %dynamic_slice.34.entry, bf16[512,1152]{1,0:T(8,128)(2,1)} %bitcast.42, f32[3,64,1152]{2,1,0:T(8,128)} %bitcast.45), custom_call_target="tpu_custom_call" | custom-call | tf_op jit(solution)/shard_map/norm/pallas_call | solution.py:69
  13.4 0.0 all-gather.5.cloned.1.call-update
  13.4 0.0 all-gather.7.cloned.1.call-start
  14.7 0.0 copy-done.7
  14.7 0.6 dynamic_slice.35
  16.6 0.0 copy-done.6
  16.6 0.1 compare_select_fusion
  16.7 0.0 copy-done.1
  16.7 0.6 gather_fusion
  17.3 0.1 and_select_fusion.coefs
  17.4 0.1 pad.16.clone
  17.5 0.1 pad.17.clone
  18.2 0.0 copy-done
  18.3 1.1 copy.22
  19.4 5.2 %constant_dynamic-slice_fusion.3 = (bf16[1,1,300,1152]{3,1,2,0:T(2,128)(2,1)}, bf16[1,1,300,1152]{3,1,2,0:T(2,128)(2,1)S(1)}) fusion(bf16[2,2,300,1152]{3,1,2,0:T(2,128)(2,1)} %param.21, s32[]{:T(128)S(6)} %select_n.44, s32[]{:T(128)S(6)} %add.42), kind=kLoop, calls=%fused_computation.11 | loop fusion | bytes 2764808 | tf_op jit(solution)/shard_map/slice | solution.py:352
  24.6 3.7 %copy.27 = bf16[1,1,300,1152]{2,3,1,0:T(8,128)(2,1)S(1)} copy(bf16[1,1,300,1152]{3,1,2,0:T(2,128)(2,1)} %get-tuple-element.25) | data formatting | bytes 1382400
  28.3 2.0 pad.12.refs_1_.refs_5_.refs_2_
  30.3 1.1 pad.14.refs_1_
  31.4 2.1 copy.26
  33.5 0.8 copy.24
  34.3 1.6 pad.13.refs_0_
  36.6 0.8 dynamic-slice_bitcast_fusion.1
  37.4 0.0 copy-done.3
  37.5 0.9 pad_maximum_fusion.refs_4_.refs_0_
  38.4 0.7 maximum_maximum_fusion.refs_6_.refs_3_
  39.1 56.2 %all-gather.5.cloned.1.call-done.refs_0_.refs_1_ = bf16[6144,1152]{1,0:T(8,128)(2,1)} async-done(((bf16[384,1152]{1,0:T(8,128)(2,1)}), bf16[6144,1152]{1,0:T(8,128)(2,1)}) %all-gather.5.cloned.1.call-update) | async-done | bytes 14155792 | tf_op jit(solution)/shard_map/all_gather | solution.py:218
  95.3 0.0 all-gather.7.cloned.1.call-update
  95.3 0.0 all-gather.9.cloned.1.call-start
  95.3 10.5 %project.2 = (bf16[6144,128]{1,0:T(8,128)(2,1)}, bf16[128,6144]{1,0:T(8,128)(2,1)}, bf16[6144,128]{1,0:T(8,128)(2,1)}) custom-call(bf16[6144,1152]{1,0:T(8,128)(2,1)} %all-gather.5.cloned.1.call-done.refs_0_.refs_1_, bf16[1152,256]{1,0:T(8,128)(2,1)} %pad.12.refs_1_.refs_5_.refs_2_), custom_call_target="tpu_custom_call" | custom-call | flops 3623878656 | bytes 18874368 | tf_op jit(solution)/shard_map/project/pallas_call | solution.py:105
  105.8 0.0 all-gather.9.cloned.1.call-update
  105.9 51.8 %self_attend.3.refs_0_.refs_4_ = f32[6144,128]{1,0:T(8,128)} custom-call(bf16[6144,128]{1,0:T(8,128)(2,1)} %get-tuple-element.16.refs_0_.refs_1_, bf16[128,6144]{1,0:T(8,128)(2,1)} %get-tuple-element.17.refs_1_.refs_2_, bf16[6144,128]{1,0:T(8,128)(2,1)} %get-tuple-element.18.refs_2_.refs_4_), custom_call_target="tpu_custom_call" | custom-call | flops 38654705664 | bytes 4194304 | tf_op jit(solution)/shard_map/self_attend/pallas_call | solution.py:194
  157.7 0.0 all-gather.7.cloned.1.call-done.refs_1_
  157.7 4.6 %project.3 = (bf16[2048,128]{1,0:T(8,128)(2,1)}, bf16[128,2048]{1,0:T(8,128)(2,1)}, bf16[2048,128]{1,0:T(8,128)(2,1)}) custom-call(f32[6144,128]{1,0:T(8,128)} %self_attend.3.refs_0_.refs_4_, bf16[2048,1152]{1,0:T(8,128)(2,1)} %all-gather.7.cloned.1.call-done.refs_1_, bf16[1152,256]{1,0:T(8,128)(2,1)} %pad.12.refs_1_.refs_5_.refs_2_), custom_call_target="tpu_custom_call" | custom-call | flops 1207959552 | bytes 6291456 | tf_op jit(solution)/shard_map/project/pallas_call | solution.py:105
  162.3 19.2 %self_attend.4.refs_0_ = bf16[16,72,384]{2,1,0:T(8,128)(2,1)} custom-call(f32[6144,128]{1,0:T(8,128)} %self_attend.3.refs_0_.refs_4_, bf16[6144,128]{1,0:T(8,128)(2,1)} %get-tuple-element.16.refs_0_.refs_1_, bf16[128,2048]{1,0:T(8,128)(2,1)} %get-tuple-element.22.refs_2_.refs_3_, bf16[2048,128]{1,0:T(8,128)(2,1)} %get-tuple-element.23.refs_3_.refs_5_, ...), custom_call_target="tpu_custom_call" | custom-call | flops 12884901888 | bytes 4194304 | tf_op jit(solution)/shard_map/self_attend/pallas_call | solution.py:194
  181.5 4.8 %all-to-all-start = ((bf16[16,72,384]{2,1,0:T(8,128)(2,1)}), bf16[16,72,384]{2,1,0:T(8,128)(2,1)S(1)}, u32[]{:S(2)}, u32[]{:S(2)}) async-start(bf16[16,72,384]{2,1,0:T(8,128)(2,1)} %self_attend.4.refs_0_), calls=%async_computation | async-start | bytes 1769472 | tf_op jit(solution)/shard_map/all_to_all | solution.py:379
  186.3 24.2 %self_attend.5.refs_0_ = bf16[16,72,128]{2,1,0:T(8,128)(2,1)} custom-call(bf16[16,72,384]{2,1,0:T(8,128)(2,1)} %self_attend.4.refs_0_, bf16[2048,128]{1,0:T(8,128)(2,1)} %get-tuple-element.24.refs_1_, bf16[128,6144]{1,0:T(8,128)(2,1)} %get-tuple-element.17.refs_1_.refs_2_, bf16[128,2048]{1,0:T(8,128)(2,1)} %get-tuple-element.22.refs_2_.refs_3_, ...), custom_call_target="tpu_custom_call" | custom-call | flops 17179869184 | bytes 4194304 | tf_op jit(solution)/shard_map/self_attend/pallas_call | solution.py:194
  210.5 0.0 all-to-all-done
  210.5 0.0 all-gather.9.cloned.1.call-done
  210.5 0.9 copy-done.2
  211.5 14.4 %all_to_all.20 = bf16[16,72,128]{2,1,0:T(8,128)(2,1)} all-to-all(bf16[16,72,128]{2,1,0:T(8,128)(2,1)} %link.7), channel_id=1, replica_groups=mesh['step'=8,'tok'=16] {'tok'}, dimensions={0} | all-to-all | bytes 589824 | tf_op jit(solution)/shard_map/all_to_all | solution.py:379
  225.8 16.9 %finish.1 = bf16[512,1152]{1,0:T(8,128)(2,1)} custom-call(bf16[1152,384]{1,0:T(8,128)(2,1)} %bitcast.38, bf16[1152,128]{1,0:T(8,128)(2,1)} %bitcast.46, bf16[512,1152]{1,0:T(8,128)(2,1)} %bitcast.43, f32[3,1152]{1,0:T(4,128)} %maximum_maximum_fusion.refs_6_.refs_3_, bf16[16,3,72,1152]{3,2,1,0:T(8,128)(2,1)} %bitcast.34, ...), custom_call_target="tpu_custom_call" | custom-call | flops 6794772480 | bytes 10485760 | tf_op jit(solution)/shard_map/finish/pallas_call | solution.py:285
  242.7 24.8 %all_to_all.21.everyone = bf16[8,64,1152]{2,1,0:T(8,128)(2,1)S(1)} all-to-all(bf16[8,64,1152]{2,1,0:T(8,128)(2,1)} %bitcast.44), channel_id=1, replica_groups=mesh['step'=8,'tok'=16] {'step'}, dimensions={0} | all-to-all | bytes 2359296 | tf_op jit(solution)/shard_map/all_to_all | solution.py:345
  267.5 0.8 scan.1
  268.3 19.8 %all_to_all.22 = bf16[8,64,1152]{2,1,0:T(8,128)(2,1)S(1)} all-to-all(bf16[8,64,1152]{2,1,0:T(8,128)(2,1)S(1)} %scan.1), channel_id=1, replica_groups=mesh['step'=8,'tok'=16] {'step'}, dimensions={0} | all-to-all | bytes 2359296 | tf_op jit(solution)/shard_map/all_to_all | solution.py:345
  288.2 1.0 copy.35
  (17 shorter events, 0.1 us)
Async XLA Ops:
  6.5 11.7 %copy-start = (bf16[2,1152,1,216]{1,3,2,0:T(8,128)(2,1)S(1)}, bf16[2,1152,1,216]{1,3,2,0:T(8,128)(2,1)}, u32[]{:S(2)}) copy-start(bf16[2,1152,1,216]{1,3,2,0:T(8,128)(2,1)} %param.17) | copy-start | bytes 2985988
  6.5 10.0 %copy-start.6 = (s32[32]{0:T(128)S(1)}, s32[32]{0:T(128)}, u32[]{:S(2)}) copy-start(s32[32]{0:T(128)} %param.12) | copy-start | bytes 388
  6.5 8.2 %copy-start.7 = (s32[32]{0:T(128)S(1)}, s32[32]{0:T(128)}, u32[]{:S(2)}) copy-start(s32[32]{0:T(128)} %param.13) | copy-start | bytes 388
  6.5 10.1 %copy-start.1 = (f32[64]{0:T(128)S(1)}, f32[64]{0:T(128)}, u32[]{:S(2)}) copy-start(f32[64]{0:T(128)} %param.16) | copy-start | bytes 772
  6.5 88.7 %all-gather.5.cloned.1.call-start = ((), (), s32[]{:S(2)}) async-start(), calls=%async_computation.4 | async-start | bytes 15040512 | tf_op jit(solution)/shard_map/all_gather | solution.py:218
  13.4 144.3 %all-gather.7.cloned.1.call-start = ((), (), s32[]{:S(2)}) async-start(), calls=%async_computation.5 | async-start | bytes 5013504 | tf_op jit(solution)/shard_map/all_gather | solution.py:218
  35.9 1.5 copy-start.3
  35.9 1.6 copy-start.4
  35.9 1.6 copy-start.5
  95.3 115.2 %all-gather.9.cloned.1.call-start = ((), (), s32[]{:S(2)}) async-start(), calls=%async_computation.6 | async-start | bytes 8460288 | tf_op jit(solution)/shard_map/all_gather | solution.py:374
  181.5 29.0 %all-to-all-start = ((bf16[16,72,384]{2,1,0:T(8,128)(2,1)}), bf16[16,72,384]{2,1,0:T(8,128)(2,1)S(1)}, u32[]{:S(2)}, u32[]{:S(2)}) async-start(bf16[16,72,384]{2,1,0:T(8,128)(2,1)} %self_attend.4.refs_0_), calls=%async_computation | async-start | bytes 1769472 | tf_op jit(solution)/shard_map/all_to_all | solution.py:379
  210.5 1.0 copy-start.2
Sparse Core Ops, SparseCore 0:
  13.5 81.7 all-gather.4
  97.0 39.4 all-gather.6
  138.2 50.1 all-gather.8
where the time goes:
time: 302 us; the launch traced here: 296 us
  Pallas kernels  133 us (44%)
  blocking collectives  59 us (20%)
  waiting for transfers between devices  56.3 us (19%)
  local copies, waits for them, and re-layouts  23.1 us (8%)
  between operations  18.1 us (6%)
  starting transfers between devices  4.96 us (2%)
    pallas_call x3, Pallas kernels, attend_chunk(): pl.pallas_call(functools.partial(attend_kernel, len(after), len(sources),...  95.1 us
    all_gather x2, waiting for transfers between devices, self_attend(): held = lax.all_gather(own, 'tok', axis=0, tiled=True)  56.2 us
    all_to_all x2, blocking collectives, over_steps(): lax.all_to_all(shaped, 'step', split_axis=0, concat_axis=0, tiled=True)  44.7 us
    pallas_call x1, Pallas kernels, finish(): pl.pallas_call(functools.partial(finish_kernel, len(turned)), grid=(1,),...  16.9 us
    pallas_call x2, Pallas kernels, project(): pl.pallas_call(functools.partial(project_kernel, len(after)), grid=(count...  15.1 us
    all_to_all x1, blocking collectives, returned(): back = lax.all_to_all(value, 'tok', split_axis=0, concat_axis=0, tiled=True)  14.4 us
    unnamed x19, local copies, waits for them, and re-layouts  7.79 us
  transfers between devices with their start and end apart: 4, of which 1 were waited for; matrix products, arithmetic and copies ran while one was open for 7% of the time, Pallas kernels for 37%

commit v1 on v0

--- a/solution.py
+++ b/solution.py
@@ -13,7 +13,7 @@
 TEXT = 300
 TEXT_PAD = 384
 CHUNKS = (384, 128)
-SOURCES = (4, 8)
+SOURCES = (2, 8)
 ROW_BLOCK = 1024
 ROWS = 128
 KEY_BLOCK = 1024
@@ -224,7 +224,13 @@
             before = states[earlier] if earlier < chunk else None
             keys = chunks[chunk : chunk + 1] if earlier < chunk else chunks[: chunk + 1]
             result = attend_chunk(
-                chunks[earlier][0], CHUNKS[earlier], SOURCES[earlier], keys, before, last, previous
+                chunks[earlier][0],
+                CHUNKS[earlier],
+                SOURCES[earlier] * (2 if earlier < chunk else 1),
+                keys,
+                before,
+                last,
+                previous,
             )
             previous = [result]
             states[earlier : earlier + 1] = [result]
@@ -381,8 +387,11 @@
 
     turned = [returned(heads_out[0])]
     turned.append(returned(link([heads_out[1]], [turned[0], all_weights])[0]))
-    sent = finish(turned, latent, mix, all_weights, text_keys, text_values)
-    return over_steps(scan(coefs, over_steps(sent))).reshape(1, count, width)
+    sent = [
+        finish([part], rows, mix, all_weights, text_keys, text_values)
+        for part, rows in zip(turned, jnp.split(latent, [CHUNKS[0]]))
+    ]
+    return over_steps(scan(coefs, over_steps(jnp.concatenate(sent, 0)))).reshape(1, count, width)
 
 
 def solution(mesh):

time: 302 us -> 308 us (1.020)
  blocking collectives: 59 us -> 46.4 us
  Pallas kernels: 133 us -> 141 us
  starting transfers between devices: 4.96 us -> 11.1 us
  local copies, waits for them, and re-layouts: 23.1 us -> 26.9 us
    all_to_all x1 -> x0, blocking collectives: 14.4 us -> none  [returned(): back = lax.all_to_all(value, 'tok', split_axis=0, concat_axis=0, tiled=True)]
    pallas_call x1 -> x2, Pallas kernels: 16.9 us -> 26.4 us  [finish(): pl.pallas_call(functools.partial(finish_kernel, len(turned)), grid=(1,),...]
    all_to_all x1 -> x2, starting transfers between devices: 4.85 us -> 10.8 us  [returned(): back = lax.all_to_all(value, 'tok', split_axis=0, concat_axis=0, tiled=True)]
    unnamed x19 -> x25, local copies, waits for them, and re-layouts: 7.79 us -> 9.88 us
  transfers between devices with their start and end apart: 4 -> 5, of which waited for: 1 -> 1; matrix products, arithmetic and copies ran while one was open for 7% -> 8% of each run, Pallas kernels for 37% -> 41%
where the time goes in v1:
time: 308 us; the launch traced here: 302 us
  Pallas kernels  141 us (46%)
  waiting for transfers between devices  56.1 us (18%)
  blocking collectives  46.4 us (15%)
  local copies, waits for them, and re-layouts  26.9 us (9%)
  between operations  18.1 us (6%)
  starting transfers between devices  11.1 us (4%)
    pallas_call x3, Pallas kernels, attend_chunk(): pl.pallas_call(functools.partial(attend_kernel, len(after), len(sources),...  93.9 us
    all_gather x2, waiting for transfers between devices, self_attend(): held = lax.all_gather(own, 'tok', axis=0, tiled=True)  56 us
    all_to_all x2, blocking collectives, over_steps(): lax.all_to_all(shaped, 'step', split_axis=0, concat_axis=0, tiled=True)  46.4 us
    pallas_call x2, Pallas kernels, finish(): pl.pallas_call(functools.partial(finish_kernel, len(turned)), grid=(1,),...  26.4 us
    pallas_call x2, Pallas kernels, project(): pl.pallas_call(functools.partial(project_kernel, len(after)), grid=(count...  15.1 us
    all_to_all x2, starting transfers between devices, returned(): back = lax.all_to_all(value, 'tok', split_axis=0, concat_axis=0, tiled=True)  10.8 us
    unnamed x25, local copies, waits for them, and re-layouts  9.88 us
  transfers between devices with their start and end apart: 5, of which 1 were waited for; matrix products, arithmetic and copies ran while one was open for 8% of the time, Pallas kernels for 41%

profile of v1, /device:TPU:0, one launch (start us, length us, event | category | flops | bytes accessed | tf_op | source)
XLA Modules:
  0.0 302.3 jit_solution(8618078099021289322)
XLA Ops:
  7.3 1.2 dynamic_slice.34.entry
  8.5 4.8 %norm.1 = (bf16[384,1152]{1,0:T(8,128)(2,1)}, bf16[128,1152]{1,0:T(8,128)(2,1)}) custom-call(s32[1]{0:T(128)} %dynamic_slice.34.entry, bf16[512,1152]{1,0:T(8,128)(2,1)} %bitcast.41, f32[3,64,1152]{2,1,0:T(8,128)} %bitcast.50), custom_call_target="tpu_custom_call" | custom-call | tf_op jit(solution)/shard_map/norm/pallas_call | solution.py:69
  13.3 0.0 all-gather.5.cloned.1.call-update
  13.3 0.0 all-gather.7.cloned.1.call-start
  14.5 0.7 dynamic_slice.35
  16.6 0.1 compare_select_fusion
  16.7 0.6 gather_fusion
  17.3 0.1 and_select_fusion.coefs
  17.4 0.1 pad.18.clone
  17.5 0.1 pad.19.clone
  18.4 1.1 copy.22
  19.4 5.1 %constant_dynamic-slice_fusion.3 = (bf16[1,1,300,1152]{3,1,2,0:T(2,128)(2,1)}, bf16[1,1,300,1152]{3,1,2,0:T(2,128)(2,1)S(1)}) fusion(bf16[2,2,300,1152]{3,1,2,0:T(2,128)(2,1)} %param.21, s32[]{:T(128)S(6)} %select_n.44, s32[]{:T(128)S(6)} %add.42), kind=kLoop, calls=%fused_computation.14 | loop fusion | bytes 2764808 | tf_op jit(solution)/shard_map/slice | solution.py:358
  24.5 3.7 %copy.27 = bf16[1,1,300,1152]{2,3,1,0:T(8,128)(2,1)S(1)} copy(bf16[1,1,300,1152]{3,1,2,0:T(2,128)(2,1)} %get-tuple-element.25) | data formatting | bytes 1382400
  28.2 2.0 pad.12.refs_1_.refs_5_.refs_2_
  30.2 1.1 pad.14.refs_1_
  31.3 2.1 copy.26
  33.4 0.9 copy.24
  34.3 1.6 pad.13.refs_0_
  36.5 0.0 copy-start.7
  36.5 0.8 dynamic-slice_bitcast_fusion.1
  37.4 0.1 copy-done.7
  37.5 0.1 copy-done.8
  37.6 0.9 pad_maximum_fusion.1.refs_4_.refs_0_
  38.5 0.7 maximum_maximum_fusion.refs_6_.refs_2_
  39.2 56.0 %all-gather.5.cloned.1.call-done.refs_0_.refs_1_ = bf16[6144,1152]{1,0:T(8,128)(2,1)} async-done(((bf16[384,1152]{1,0:T(8,128)(2,1)}), bf16[6144,1152]{1,0:T(8,128)(2,1)}) %all-gather.5.cloned.1.call-update) | async-done | bytes 14155792 | tf_op jit(solution)/shard_map/all_gather | solution.py:218
  95.2 0.0 all-gather.7.cloned.1.call-update
  95.2 0.2 all-gather.9.cloned.1.call-start
  95.4 10.5 %project.2 = (bf16[6144,128]{1,0:T(8,128)(2,1)}, bf16[128,6144]{1,0:T(8,128)(2,1)}, bf16[6144,128]{1,0:T(8,128)(2,1)}) custom-call(bf16[6144,1152]{1,0:T(8,128)(2,1)} %all-gather.5.cloned.1.call-done.refs_0_.refs_1_, bf16[1152,256]{1,0:T(8,128)(2,1)} %pad.12.refs_1_.refs_5_.refs_2_), custom_call_target="tpu_custom_call" | custom-call | flops 3623878656 | bytes 18874368 | tf_op jit(solution)/shard_map/project/pallas_call | solution.py:105
  106.0 0.0 all-gather.9.cloned.1.call-update
  106.0 1.2 copy-done.2
  107.2 0.8 slice_bitcast_fusion.1.refs_1_
  108.0 1.0 slice_bitcast_fusion.refs_1_
  109.0 50.6 %self_attend.3.refs_0_.refs_4_ = f32[6144,128]{1,0:T(8,128)} custom-call(bf16[6144,128]{1,0:T(8,128)(2,1)} %get-tuple-element.16.refs_0_.refs_1_, bf16[128,6144]{1,0:T(8,128)(2,1)} %get-tuple-element.17.refs_1_.refs_2_, bf16[6144,128]{1,0:T(8,128)(2,1)} %get-tuple-element.18.refs_2_.refs_4_), custom_call_target="tpu_custom_call" | custom-call | flops 38654705664 | bytes 4194304 | tf_op jit(solution)/shard_map/self_attend/pallas_call | solution.py:194
  159.6 4.5 %project.3 = (bf16[2048,128]{1,0:T(8,128)(2,1)}, bf16[128,2048]{1,0:T(8,128)(2,1)}, bf16[2048,128]{1,0:T(8,128)(2,1)}) custom-call(f32[6144,128]{1,0:T(8,128)} %self_attend.3.refs_0_.refs_4_, bf16[2048,1152]{1,0:T(8,128)(2,1)} %all-gather.7.cloned.1.call-done.refs_1_, bf16[1152,256]{1,0:T(8,128)(2,1)} %pad.12.refs_1_.refs_5_.refs_2_), custom_call_target="tpu_custom_call" | custom-call | flops 1207959552 | bytes 6291456 | tf_op jit(solution)/shard_map/project/pallas_call | solution.py:105
  164.1 19.2 %self_attend.4.refs_0_ = bf16[16,72,384]{2,1,0:T(8,128)(2,1)} custom-call(f32[6144,128]{1,0:T(8,128)} %self_attend.3.refs_0_.refs_4_, bf16[6144,128]{1,0:T(8,128)(2,1)} %get-tuple-element.16.refs_0_.refs_1_, bf16[128,2048]{1,0:T(8,128)(2,1)} %get-tuple-element.22.refs_2_.refs_3_, bf16[2048,128]{1,0:T(8,128)(2,1)} %get-tuple-element.23.refs_3_.refs_5_, ...), custom_call_target="tpu_custom_call" | custom-call | flops 12884901888 | bytes 4194304 | tf_op jit(solution)/shard_map/self_attend/pallas_call | solution.py:194
  183.3 4.9 %all-to-all-start = ((bf16[16,72,384]{2,1,0:T(8,128)(2,1)}), bf16[16,72,384]{2,1,0:T(8,128)(2,1)S(1)}, u32[]{:S(2)}, u32[]{:S(2)}) async-start(bf16[16,72,384]{2,1,0:T(8,128)(2,1)} %self_attend.4.refs_0_), calls=%async_computation | async-start | bytes 1769472 | tf_op jit(solution)/shard_map/all_to_all | solution.py:385
  188.2 24.1 %self_attend.5.refs_0_ = bf16[16,72,128]{2,1,0:T(8,128)(2,1)} custom-call(bf16[16,72,384]{2,1,0:T(8,128)(2,1)} %self_attend.4.refs_0_, bf16[2048,128]{1,0:T(8,128)(2,1)} %get-tuple-element.24.refs_1_, bf16[128,6144]{1,0:T(8,128)(2,1)} %get-tuple-element.17.refs_1_.refs_2_, bf16[128,2048]{1,0:T(8,128)(2,1)} %get-tuple-element.22.refs_2_.refs_3_, ...), custom_call_target="tpu_custom_call" | custom-call | flops 17179869184 | bytes 4194304 | tf_op jit(solution)/shard_map/self_attend/pallas_call | solution.py:194
  212.4 0.0 all-gather.9.cloned.1.call-done
  212.4 0.9 copy-done.3
  213.3 5.9 %all-to-all-start.1 = ((bf16[16,72,128]{2,1,0:T(8,128)(2,1)}), bf16[16,72,128]{2,1,0:T(8,128)(2,1)S(1)}, u32[]{:S(2)}, u32[]{:S(2)}) async-start(bf16[16,72,128]{2,1,0:T(8,128)(2,1)} %link.7), calls=%async_computation.1 | async-start | bytes 589824 | tf_op jit(solution)/shard_map/all_to_all | solution.py:385
  219.1 15.6 %finish.2 = bf16[384,1152]{1,0:T(8,128)(2,1)} custom-call(bf16[1152,384]{1,0:T(8,128)(2,1)} %bitcast.45, bf16[384,1152]{1,0:T(8,128)(2,1)} %slice_bitcast_fusion.refs_1_, f32[3,1152]{1,0:T(4,128)} %maximum_maximum_fusion.refs_6_.refs_2_, bf16[16,3,72,1152]{3,2,1,0:T(8,128)(2,1)} %bitcast.38, bf16[16,384,72]{2,1,0:T(8,128)(2,1)} %get-tuple-element.20.refs_2_.refs_4_, ...), custom_call_target="tpu_custom_call" | custom-call | flops 5096079360 | bytes 10485760 | tf_op jit(solution)/shard_map/finish/pallas_call | solution.py:291
  234.7 0.7 copy-done.4
  235.4 10.8 %finish.3 = bf16[128,1152]{1,0:T(8,128)(2,1)} custom-call(bf16[1152,128]{1,0:T(8,128)(2,1)} %bitcast.49, bf16[128,1152]{1,0:T(8,128)(2,1)} %slice_bitcast_fusion.1.refs_1_, f32[3,1152]{1,0:T(4,128)} %maximum_maximum_fusion.refs_6_.refs_2_, bf16[16,3,72,1152]{3,2,1,0:T(8,128)(2,1)} %bitcast.39, bf16[16,384,72]{2,1,0:T(8,128)(2,1)} %get-tuple-element.20.refs_2_.refs_4_, ...), custom_call_target="tpu_custom_call" | custom-call | flops 1698693120 | bytes 10485760 | tf_op jit(solution)/shard_map/finish/pallas_call | solution.py:291
  246.3 1.1 pad_maximum_fusion
  247.4 25.6 %all_to_all.20.everyone = bf16[8,64,1152]{2,1,0:T(8,128)(2,1)S(1)} all-to-all(bf16[8,64,1152]{2,1,0:T(8,128)(2,1)S(1)} %bitcast.42), channel_id=1, replica_groups=mesh['step'=8,'tok'=16] {'step'}, dimensions={0} | all-to-all | bytes 2359296 | tf_op jit(solution)/shard_map/all_to_all | solution.py:351
  273.0 0.8 scan.1
  273.8 20.7 %all_to_all.21 = bf16[8,64,1152]{2,1,0:T(8,128)(2,1)S(1)} all-to-all(bf16[8,64,1152]{2,1,0:T(8,128)(2,1)S(1)} %scan.1), channel_id=1, replica_groups=mesh['step'=8,'tok'=16] {'step'}, dimensions={0} | all-to-all | bytes 2359296 | tf_op jit(solution)/shard_map/all_to_all | solution.py:351
  294.5 1.0 copy.35
  (28 shorter events, 0.2 us)
Async XLA Ops:
  6.5 11.8 %copy-start = (bf16[2,1152,1,216]{1,3,2,0:T(8,128)(2,1)S(1)}, bf16[2,1152,1,216]{1,3,2,0:T(8,128)(2,1)}, u32[]{:S(2)}) copy-start(bf16[2,1152,1,216]{1,3,2,0:T(8,128)(2,1)} %param.17) | copy-start | bytes 2985988
  6.5 88.6 %all-gather.5.cloned.1.call-start = ((), (), s32[]{:S(2)}) async-start(), calls=%async_computation.4 | async-start | bytes 15040512 | tf_op jit(solution)/shard_map/all_gather | solution.py:218
  8.5 6.0 %copy-start.10 = (s32[32]{0:T(128)S(1)}, s32[32]{0:T(128)}, u32[]{:S(2)}) copy-start(s32[32]{0:T(128)} %param.13) | copy-start | bytes 388
  8.5 8.0 %copy-start.9 = (s32[32]{0:T(128)S(1)}, s32[32]{0:T(128)}, u32[]{:S(2)}) copy-start(s32[32]{0:T(128)} %param.12) | copy-start | bytes 388
  8.5 8.1 %copy-start.1 = (f32[64]{0:T(128)S(1)}, f32[64]{0:T(128)}, u32[]{:S(2)}) copy-start(f32[64]{0:T(128)} %param.16) | copy-start | bytes 772
  13.3 146.3 %all-gather.7.cloned.1.call-start = ((), (), s32[]{:S(2)}) async-start(), calls=%async_computation.5 | async-start | bytes 5013504 | tf_op jit(solution)/shard_map/all_gather | solution.py:218
  35.9 1.5 copy-start.6
  36.5 1.0 copy-start.7
  36.5 1.1 copy-start.8
  95.2 117.2 %all-gather.9.cloned.1.call-start = ((), (), s32[]{:S(2)}) async-start(), calls=%async_computation.6 | async-start | bytes 8460288 | tf_op jit(solution)/shard_map/all_gather | solution.py:380
  106.0 1.3 copy-start.2
  183.3 29.0 %all-to-all-start = ((bf16[16,72,384]{2,1,0:T(8,128)(2,1)}), bf16[16,72,384]{2,1,0:T(8,128)(2,1)S(1)}, u32[]{:S(2)}, u32[]{:S(2)}) async-start(bf16[16,72,384]{2,1,0:T(8,128)(2,1)} %self_attend.4.refs_0_), calls=%async_computation | async-start | bytes 1769472 | tf_op jit(solution)/shard_map/all_to_all | solution.py:385
  212.3 0.9 copy-start.3
  213.3 21.4 %all-to-all-start.1 = ((bf16[16,72,128]{2,1,0:T(8,128)(2,1)}), bf16[16,72,128]{2,1,0:T(8,128)(2,1)S(1)}, u32[]{:S(2)}, u32[]{:S(2)}) async-start(bf16[16,72,128]{2,1,0:T(8,128)(2,1)} %link.7), calls=%async_computation.1 | async-start | bytes 589824 | tf_op jit(solution)/shard_map/all_to_all | solution.py:385
  234.7 0.7 copy-start.4
  235.4 10.9 %copy-start.5 = (bf16[384,1152]{1,0:T(8,128)(2,1)S(1)}, bf16[384,1152]{1,0:T(8,128)(2,1)}, u32[]{:S(2)}) copy-start(bf16[384,1152]{1,0:T(8,128)(2,1)} %finish.2) | copy-start | bytes 2654212
Sparse Core Ops, SparseCore 0:
  13.4 81.7 all-gather.4
  96.9 39.5 all-gather.6
  138.2 50.1 all-gather.8
